TPU v7x, 256 devices: a whole 4x4x8 slice. The times are simulated.
256 devices in a mesh: dp: 32 (over x, y, core), tensor: 8 (over z).
Axes of the slice: x: 4, y: 4, z: 8, core: 2. Of those that a mesh axis runs over, the one named last changes fastest.
Arguments:
- patches: bfloat16 [32768, 1280], P('dp'), may hold values from -6 to 6
- vit_gain: float32 [1280], replicated, may hold values from 0.5 to 1.5
- fc_in: bfloat16 [1280, 5120], P(None, 'tensor'), may hold values from -0.15625 to 0.15625
- fc_out: bfloat16 [5120, 1280], P('tensor'), may hold values from -0.078125 to 0.078125
- merge_gain: float32 [1280], replicated, may hold values from 0.5 to 1.5
- merge_shift: float32 [1280], replicated, may hold values from -3 to 3
- merger: bfloat16 [5120, 8192], P('dp', 'tensor'), may hold values from -0.078125 to 0.078125
- counts: int32 [32, 32], replicated, may hold values from 0 to 16, as said below
- grad_packed: bfloat16 [16384, 8192], P('dp', 'tensor'), may hold values from -6 to 6
Outputs:
- visual: bfloat16 [16384, 8192], P('dp', 'tensor')
- grad_weight: float32 [5120, 8192], P('dp', 'tensor')
- grad_layer: float32 [32768, 1280], P(('dp', 'tensor'))
Inputs may be any that keep to these rules, and one draw needn't show every extreme that they name: counts[s, d] is the number of merged tokens that dp index s sends to dp index d, taken in order from s's 256 tokens; every row sums to 256 and holds the value 16 at least once.
All inputs are finite; a program needn't handle non-finite values.
Results may differ from a plain program's by a relative error of at most 0.023.
Values may be sent and summed in bfloat16 or wider, within the bound.
No kernel may reach another device: no remote copies, remote signals or barrier semaphores. Data moves between devices by JAX's collectives and lax.ppermute only.
A program may use at most 128 MiB of HBM per device.

v0:
```python
import math

import jax
import jax.numpy as jnp
from jax import lax
from jax.sharding import PartitionSpec as P

epsilon = 1e-06


def layer_norm(values, gain, shift):
    average = jnp.mean(values, axis=-1, keepdims=True)
    centered = values - average
    variance = jnp.mean(centered * centered, axis=-1, keepdims=True)
    return centered * lax.rsqrt(variance + epsilon) * gain + shift


def quick_gelu(values):
    return values * jax.nn.sigmoid(1.702 * values)


def exclusive_sum(values):
    return jnp.cumsum(values) - values


def body(patches, vit_gain, fc_in, fc_out, merge_gain, merge_shift, merger, counts, grad_packed):
    tensor_size = lax.axis_size("tensor")
    dp_size = lax.axis_size("dp")
    tensor_rank = lax.axis_index("tensor")
    dp_rank = lax.axis_index("dp")
    patch_rows = patches.shape[0]
    my_rows = patch_rows // tensor_size
    width = patches.shape[1]
    merged_width = 4 * width
    tokens = patch_rows // 4
    inputs = patches.astype(jnp.float32)
    normed = layer_norm(inputs, vit_gain, 0.0).astype(jnp.bfloat16)
    hidden = quick_gelu(jnp.dot(normed, fc_in, preferred_element_type=jnp.float32)).astype(
        jnp.bfloat16
    )
    summed = lax.psum_scatter(
        jnp.dot(hidden, fc_out, preferred_element_type=jnp.float32).astype(jnp.bfloat16),
        "tensor",
        scatter_dimension=0,
        tiled=True,
    ).astype(jnp.float32)
    layer_out = lax.dynamic_slice_in_dim(inputs, tensor_rank * my_rows, my_rows, 0) + summed
    normed_mine = layer_norm(layer_out, merge_gain, merge_shift).astype(jnp.bfloat16)
    merged = lax.all_gather(
        normed_mine.reshape(my_rows // 4, merged_width), "tensor", axis=0, tiled=True
    )
    full_weight = lax.all_gather(merger, "dp", axis=0, tiled=True)
    projected = jnp.dot(merged, full_weight, preferred_element_type=jnp.float32)
    projected = projected.astype(jnp.bfloat16)
    capacity = 2 * tokens // dp_size
    packed_rows = dp_size * capacity
    send_counts = lax.dynamic_index_in_dim(counts, dp_rank, 0, keepdims=False)
    recv_counts = lax.dynamic_index_in_dim(counts, dp_rank, 1, keepdims=False)
    send_start = exclusive_sum(send_counts)
    recv_start = exclusive_sum(recv_counts)
    slot_index = jnp.arange(capacity, dtype=jnp.int32)
    send_valid = slot_index[None, :] < send_counts[:, None]
    send_rows = jnp.clip(send_start[:, None] + slot_index[None, :], 0, tokens - 1)
    outgoing = jnp.where(send_valid[:, :, None], projected[send_rows], jnp.zeros((), jnp.bfloat16))
    incoming = lax.all_to_all(outgoing, "dp", split_axis=0, concat_axis=0, tiled=True).reshape(
        packed_rows, -1
    )
    position = jnp.arange(packed_rows, dtype=jnp.int32)
    source = jnp.sum(
        ((recv_start + recv_counts)[None, :] <= position[:, None]).astype(jnp.int32), axis=1
    )
    source = jnp.minimum(source, dp_size - 1)
    placed_valid = position < jnp.sum(recv_counts)
    flat_index = jnp.clip(source * capacity + position - recv_start[source], 0, packed_rows - 1)
    visual = jnp.where(placed_valid[:, None], incoming[flat_index], jnp.zeros((), jnp.bfloat16))
    back_valid = slot_index[None, :] < recv_counts[:, None]
    back_rows = jnp.clip(recv_start[:, None] + slot_index[None, :], 0, packed_rows - 1)
    returning = jnp.where(
        back_valid[:, :, None], grad_packed[back_rows], jnp.zeros((), jnp.bfloat16)
    )
    arrived = lax.all_to_all(returning, "dp", split_axis=0, concat_axis=0, tiled=True).reshape(
        packed_rows, -1
    )
    token_index = jnp.arange(tokens, dtype=jnp.int32)
    target = jnp.sum(
        ((send_start + send_counts)[None, :] <= token_index[:, None]).astype(jnp.int32), axis=1
    )
    target = jnp.minimum(target, dp_size - 1)
    token_grads = arrived[target * capacity + token_index - send_start[target]]
    grad_scale = 1.0 / math.sqrt(tokens * dp_size)
    grad_weight = lax.psum_scatter(
        (
            lax.dot_general(
                merged, token_grads, (((0,), (0,)), ((), ())), preferred_element_type=jnp.float32
            )
            * grad_scale
        ).astype(jnp.bfloat16),
        "dp",
        scatter_dimension=0,
        tiled=True,
    ).astype(jnp.float32)
    merged_grads = lax.psum_scatter(
        lax.dot_general(
            token_grads, full_weight, (((1,), (1,)), ((), ())), preferred_element_type=jnp.float32
        ).astype(jnp.bfloat16),
        "tensor",
        scatter_dimension=0,
        tiled=True,
    ).astype(jnp.float32)
    merged_grads = merged_grads.reshape(my_rows, width)
    average = jnp.mean(layer_out, axis=-1, keepdims=True)
    centered = layer_out - average
    inverse = lax.rsqrt(jnp.mean(centered * centered, axis=-1, keepdims=True) + epsilon)
    normal = centered * inverse
    scaled = merged_grads * merge_gain
    grad_layer = inverse * (
        scaled
        - jnp.mean(scaled, axis=-1, keepdims=True)
        - normal * jnp.mean(scaled * normal, axis=-1, keepdims=True)
    )
    return (visual, grad_weight, grad_layer)


def solution(mesh):
    in_specs = (
        P("dp", None),
        P(),
        P(None, "tensor"),
        P("tensor", None),
        P(),
        P(),
        P("dp", "tensor"),
        P(),
        P("dp", "tensor"),
    )
    out_specs = (P("dp", "tensor"), P("dp", "tensor"), P(("dp", "tensor"), None))
    return jax.shard_map(body, mesh=mesh, in_specs=in_specs, out_specs=out_specs, check_vma=False)
```

profile of v0, /device:TPU:1, one launch (start us, length us, event | category | flops | bytes accessed | tf_op | source)
XLA Modules:
  0.0 310.6 jit_solution(5462260340332964187)
XLA Ops:
  8.8 2.3 convert_reduce_fusion
  12.2 7.7 %convolution_convert_fusion.1 = bf16[1024,1280]{1,0:T(8,128)(2,1)} fusion(bf16[640,1280]{1,0:T(8,128)(2,1)S(1)} %copy-done, bf16[1280,640]{1,0:T(8,128)(2,1)S(1)} %copy-done.7, bf16[1024,1280]{1,0:T(8,128)(2,1)} %param.9, f32[1280]{0:T(1024)S(1)} %copy-done.8, f32[1024]{0:T(1024)S(1)} %add_rsqrt_fusion, f32[1024]{0:T(1024)S(1)} %broadcast_multiply_fusion), kind=kOutput, calls=%fused_computation.9 | convolution fusion | flops 3367239680 | bytes 8532992 | tf_op jit(solution)/shard_map/dot_general | solution.py:42
  21.7 2.8 gather_fusion.2
  24.6 2.3 broadcast_select_fusion.1
  26.9 8.6 %all-to-all-start.1 = ((bf16[32,16,1024]{2,1,0:T(8,128)(2,1)}), bf16[32,16,1024]{2,1,0:T(8,128)(2,1)S(1)}, u32[]{:S(2)}, u32[]{:S(2)}) async-start(bf16[32,16,1024]{2,1,0:T(8,128)(2,1)} %broadcast_select_fusion.1), calls=%async_computation.2 | async-start | bytes 2097152 | tf_op jit(solution)/shard_map/all_to_all | solution.py:81
  37.4 4.4 %compare_select_fusion.12 = (s32[256,1]{0,1:T(1,128)S(1)}, s32[256,1]{0,1:T(1,128)S(1)}) fusion(s32[]{:T(128)} %bitcast.68, s32[]{:T(128)} %bitcast.69, s32[]{:T(128)} %bitcast.70, s32[]{:T(128)} %bitcast.71, s32[]{:T(128)} %bitcast.72, s32[]{:T(128)} %bitcast.74, s32[]{:T(128)} %bitcast.73, s32[256,1]{0,1:T(1,128)S(1)} %bitcast.99), kind=kLoop, calls=%fused_computation.102 | loop fusion | flops 3840 | bytes 3100 | tf_op jit(solution)/shard_map/gather | solution.py:89
  42.0 15.7 %select_select_fusion.1 = s32[256]{0:T(256)S(1)} fusion(pred[256]{0:T(512)(128)(4,1)S(1)} %get-tuple-element.58, pred[256]{0:T(512)(128)(4,1)S(1)} %get-tuple-element.57, pred[256]{0:T(512)(128)(4,1)S(1)} %get-tuple-element.56, pred[256]{0:T(512)(128)(4,1)S(1)} %get-tuple-element.55, pred[256]{0:T(512)(128)(4,1)S(1)} %get-tuple-element.54, ...), kind=kLoop, calls=%fused_computation.111 | loop fusion | flops 6400 | bytes 8548 | tf_op jit(solution)/shard_map/gather | solution.py:89
  57.7 1.2 gather_fusion.3
  58.9 29.5 %all-gather.5.cloned.1.call-done = bf16[5120,1024]{1,0:T(8,128)(2,1)} async-done(((bf16[160,1024]{1,0:T(8,128)(2,1)}), bf16[5120,1024]{1,0:T(8,128)(2,1)}) %all-gather.5.cloned.1.call-update) | async-done | bytes 10485776 | tf_op jit(solution)/shard_map/all_gather | solution.py:52
  88.4 12.2 %convolution_convert_fusion = bf16[256,5120]{1,0:T(8,128)(2,1)} fusion(bf16[256,1024]{1,0:T(8,128)(2,1)S(1)} %gather_fusion.3, bf16[5120,1024]{1,0:T(8,128)(2,1)} %all-gather.5.cloned.1.call-done), kind=kOutput, calls=%fused_computation.5 | convolution fusion | flops 2685665280 | bytes 13631488 | tf_op jit(solution)/shard_map/dot_general | solution.py:103
  100.9 4.5 %convert_element_type.37 = f32[1024,1280]{1,0:T(8,128)} convert(bf16[1024,1280]{1,0:T(8,128)(2,1)} %param.9) | non-fusion elementwise | flops 1310720 | bytes 7864320 | tf_op jit(solution)/shard_map/convert_element_type | solution.py:36
  105.4 1.4 fusion.12
  107.0 32.8 %reduce-scatter.8.cloned.1.call-done = bf16[32,5120]{1,0:T(8,128)(2,1)} async-done(((bf16[256,5120]{1,0:T(8,128)(2,1)}), bf16[32,5120]{1,0:T(8,128)(2,1)}) %reduce-scatter.8.cloned.1.call-update) | async-done | bytes 327696 | tf_op jit(solution)/shard_map/reduce_scatter | solution.py:102
  143.3 42.9 %all-gather.3.cloned.1.call-done = bf16[256,5120]{1,0:T(8,128)(2,1)} async-done(((bf16[32,5120]{1,0:T(8,128)(2,1)}), bf16[256,5120]{1,0:T(8,128)(2,1)}) %all-gather.3.cloned.1.call-update) | async-done | bytes 2621456 | tf_op jit(solution)/shard_map/all_gather | solution.py:49
  186.2 8.6 %multiply_convert_fusion = bf16[5120,1024]{1,0:T(8,128)(2,1)} fusion(bf16[256,5120]{1,0:T(8,128)(2,1)} %all-gather.3.cloned.1.call-done, bf16[256,1024]{1,0:T(8,128)(2,1)} %copy-done.3), kind=kOutput, calls=%fused_computation.4 | convolution fusion | flops 2694840320 | bytes 13631488 | tf_op jit(solution)/shard_map/dot_general | solution.py:93
  196.6 7.6 %convolution_convert_fusion.2 = bf16[256,1024]{1,0:T(8,128)(2,1)S(1)} fusion(bf16[256,5120]{1,0:T(8,128)(2,1)} %all-gather.3.cloned.1.call-done, bf16[5120,1024]{1,0:T(8,128)(2,1)} %all-gather.5.cloned.1.call-done), kind=kOutput, calls=%fused_computation.17 | convolution fusion | flops 2684616704 | bytes 13631488 | tf_op jit(solution)/shard_map/dot_general | solution.py:53
  204.2 2.1 gather_fusion
  207.4 10.5 %all-to-all-start = ((bf16[32,16,1024]{2,1,0:T(8,128)(2,1)}), bf16[32,16,1024]{2,1,0:T(8,128)(2,1)S(1)}, u32[]{:S(2)}, u32[]{:S(2)}) async-start(bf16[32,16,1024]{2,1,0:T(8,128)(2,1)} %broadcast_select_fusion.2), calls=%async_computation.1 | async-start | bytes 2097152 | tf_op jit(solution)/shard_map/all_to_all | solution.py:65
  218.6 4.2 %compare_select_fusion.4 = (s32[512,1]{0,1:T(1,128)S(1)}, s32[512,1]{0,1:T(1,128)S(1)}) fusion(s32[]{:T(128)} %bitcast.30, s32[]{:T(128)} %bitcast.31, s32[]{:T(128)} %bitcast.32, s32[]{:T(128)} %bitcast.33, s32[]{:T(128)} %bitcast.34, s32[]{:T(128)} %bitcast.36, s32[]{:T(128)} %bitcast.35, s32[512,1]{0,1:T(1,128)S(1)} %bitcast.97), kind=kLoop, calls=%fused_computation.64 | loop fusion | flops 7680 | bytes 6172 | tf_op jit(solution)/shard_map/gather | solution.py:74
  223.0 16.0 %select_select_fusion = s32[512]{0:T(512)S(1)} fusion(pred[512]{0:T(512)(128)(4,1)S(1)} %get-tuple-element.33, pred[512]{0:T(512)(128)(4,1)S(1)} %get-tuple-element.32, pred[512]{0:T(512)(128)(4,1)S(1)} %get-tuple-element.31, pred[512]{0:T(512)(128)(4,1)S(1)} %get-tuple-element.30, pred[512]{0:T(512)(128)(4,1)S(1)} %get-tuple-element.29, ...), kind=kLoop, calls=%fused_computation.108 | loop fusion | flops 12800 | bytes 16996 | tf_op jit(solution)/shard_map/gather | solution.py:74
  239.1 2.8 gather_fusion.1
  241.9 2.3 broadcast_select_fusion
  244.2 56.9 %reduce-scatter.6.cloned.1.call-done = bf16[160,1024]{1,0:T(8,128)(2,1)} async-done(((bf16[5120,1024]{1,0:T(8,128)(2,1)}), bf16[160,1024]{1,0:T(8,128)(2,1)}) %reduce-scatter.6.cloned.1.call-update) | async-done | bytes 327696 | tf_op jit(solution)/shard_map/reduce_scatter | solution.py:91
  301.2 1.9 convert_element_type.47
  (75 shorter events, 13.5 us)
Async XLA Ops:
  8.0 4.2 %copy-start = (bf16[640,1280]{1,0:T(8,128)(2,1)S(1)}, bf16[640,1280]{1,0:T(8,128)(2,1)}, u32[]{:S(2)}) copy-start(bf16[640,1280]{1,0:T(8,128)(2,1)} %param.12) | copy-start | bytes 4915204
  8.0 80.4 %all-gather.5.cloned.1.call-start = ((), (), s32[]{:S(2)}) async-start(), calls=%async_computation.7 | async-start | bytes 10813440 | tf_op jit(solution)/shard_map/all_gather | solution.py:52
  8.7 3.4 %copy-start.8 = (f32[1280]{0:T(1024)S(1)}, f32[1280]{0:T(1024)}, u32[]{:S(2)}) copy-start(f32[1280]{0:T(1024)} %param.10) | copy-start | bytes 15364
  8.8 96.6 %reduce-scatter.4.cloned.1.call-start = ((), (), s32[]{:S(2)}) async-start(), calls=%async_computation.5 | async-start | bytes 2949120 | tf_op jit(solution)/shard_map/reduce_scatter | solution.py:41
  8.8 2.5 copy-start.2
  8.8 3.4 %copy-start.7 = (bf16[1280,640]{1,0:T(8,128)(2,1)S(1)}, bf16[1280,640]{1,0:T(8,128)(2,1)}, u32[]{:S(2)}) copy-start(bf16[1280,640]{1,0:T(8,128)(2,1)} %param.11) | copy-start | bytes 4915204
  19.9 0.7 copy-start.4
  19.9 1.8 copy-start.1
  26.9 30.8 %all-to-all-start.1 = ((bf16[32,16,1024]{2,1,0:T(8,128)(2,1)}), bf16[32,16,1024]{2,1,0:T(8,128)(2,1)S(1)}, u32[]{:S(2)}, u32[]{:S(2)}) async-start(bf16[32,16,1024]{2,1,0:T(8,128)(2,1)} %broadcast_select_fusion.1), calls=%async_computation.2 | async-start | bytes 2097152 | tf_op jit(solution)/shard_map/all_to_all | solution.py:81
  35.5 104.2 %reduce-scatter.8.cloned.1.call-start = ((), (), s32[]{:S(2)}) async-start(), calls=%async_computation.9 | async-start | bytes 2949120 | tf_op jit(solution)/shard_map/reduce_scatter | solution.py:102
  58.9 41.7 %copy-start.3 = (bf16[256,1024]{1,0:T(8,128)(2,1)}, bf16[256,1024]{1,0:T(8,128)(2,1)S(1)}, u32[]{:S(2)}) copy-start(bf16[256,1024]{1,0:T(8,128)(2,1)S(1)} %gather_fusion.3) | copy-start | bytes 1572868
  100.6 85.5 %all-gather.3.cloned.1.call-start = ((), (), s32[]{:S(2)}) async-start(), calls=%async_computation.6 | async-start | bytes 2949120 | tf_op jit(solution)/shard_map/all_gather | solution.py:49
  105.4 35.5 %copy-start.5 = (f32[1280]{0:T(1024)S(1)}, f32[1280]{0:T(1024)}, u32[]{:S(2)}) copy-start(f32[1280]{0:T(1024)} %param.13) | copy-start | bytes 15364
  105.4 35.8 %copy-start.6 = (f32[1280]{0:T(1024)S(1)}, f32[1280]{0:T(1024)}, u32[]{:S(2)}) copy-start(f32[1280]{0:T(1024)} %param.14) | copy-start | bytes 15364
  143.2 157.9 %reduce-scatter.6.cloned.1.call-start = ((), (), s32[]{:S(2)}) async-start(), calls=%async_computation.8 | async-start | bytes 10813440 | tf_op jit(solution)/shard_map/reduce_scatter | solution.py:91
  207.4 31.7 %all-to-all-start = ((bf16[32,16,1024]{2,1,0:T(8,128)(2,1)}), bf16[32,16,1024]{2,1,0:T(8,128)(2,1)S(1)}, u32[]{:S(2)}, u32[]{:S(2)}) async-start(bf16[32,16,1024]{2,1,0:T(8,128)(2,1)} %broadcast_select_fusion.2), calls=%async_computation.1 | async-start | bytes 2097152 | tf_op jit(solution)/shard_map/all_to_all | solution.py:65
Sparse Core Ops, SparseCore 0:
  11.4 76.9 all-gather.4
  194.9 106.2 reduce-scatter.5
Sparse Core Ops, SparseCore 1:
  20.0 43.4 reduce-scatter.3
  100.7 38.9 reduce-scatter.7
  143.3 42.8 all-gather.2
where the time goes:
time: 312 us; the launch traced here: 311 us
  waiting for transfers between devices  163 us (52%)
  other arithmetic  61.2 us (20%)
  matrix products  36.1 us (12%)
  starting transfers between devices  19.5 us (6%)
  between operations  15.9 us (5%)
  local copies, waits for them, and re-layouts  15 us (5%)
    reduce_scatter x1, waiting for transfers between devices, body(): lax.psum_scatter((lax.dot_general(merged, token_grads, (((0,), (0,)), (()...  56.9 us
    all_gather x1, waiting for transfers between devices, body(): lax.all_gather(normed_mine.reshape(my_rows // 4, merged_width), 'tensor',...  42.9 us
    reduce_scatter x1, waiting for transfers between devices, body(): lax.psum_scatter(lax.dot_general(token_grads, full_weight, (((1,), (1,)),...  32.8 us
    all_gather x1, waiting for transfers between devices, body(): full_weight = lax.all_gather(merger, 'dp', axis=0, tiled=True)  29.5 us
    gather x3, other arithmetic, body(): recv_start[source]  20.4 us
    gather x4, other arithmetic, body(): token_grads = arrived[target * capacity + token_index - send_start[target]]  20.3 us
    dot_general x1, matrix products, body(): lax.dot_general(token_grads, full_weight, (((1,), (1,)), ((), ())), prefe...  12.2 us
    all_to_all x1, starting transfers between devices, body(): lax.all_to_all(outgoing, 'dp', split_axis=0, concat_axis=0, tiled=True)  10.5 us
  transfers between devices with their start and end apart: 7, of which 4 were waited for; matrix products, arithmetic and copies ran while one was open for 31% of the time, Pallas kernels for 0%

commit v1 on v0

v1 whole, which is shorter than its diff:
```python
import math

import jax
import jax.numpy as jnp
from jax import lax
from jax.sharding import Mesh
from jax.sharding import PartitionSpec as P

epsilon = 1e-06
bf16 = jnp.bfloat16
f32 = jnp.float32
DP = ("x", "y", "c")
SWAP = [(0, 1), (1, 0)]


def layer_norm(values, gain, shift):
    average = jnp.mean(values, axis=-1, keepdims=True)
    centered = values - average
    variance = jnp.mean(centered * centered, axis=-1, keepdims=True)
    return centered * lax.rsqrt(variance + epsilon) * gain + shift


def quick_gelu(values):
    return values * jax.nn.sigmoid(1.702 * values)


def exclusive_sum(values):
    return jnp.cumsum(values) - values


def position(x, y, c):
    return ((x % 4) * 4 + (y % 4)) * 2 + c


def ring_pairs(axis):
    pairs = []
    for x in range(4):
        for y in range(4):
            for c in range(2):
                step = 1 - 2 * c
                to = position(x + step, y, c) if axis == "x" else position(x, y + step, c)
                pairs.append((position(x, y, c), to))
    return pairs


def pick(array, index, axis):
    return lax.dynamic_index_in_dim(array, index % 4, axis, keepdims=False)


def scatter_chips(parts):
    place = {"x": lax.axis_index("x"), "y": lax.axis_index("y")}
    sign = 1 - 2 * lax.axis_index("c")
    dim = {"x": 0, "y": 1}
    pairs = {"x": ring_pairs("x"), "y": ring_pairs("y")}
    running = [pick(a, place[ax] - sign, dim[ax]) for ax, a in parts]
    for step in range(3):
        for i, (ax, a) in enumerate(parts):
            came = lax.ppermute(running[i], DP, pairs[ax])
            mine = pick(a, place[ax] - sign * (2 + step), dim[ax])
            running[i] = (came.astype(f32) + mine.astype(f32)).astype(bf16)
    sums = []
    for i, (ax, _) in enumerate(parts):
        other = "y" if ax == "x" else "x"
        total = pick(running[i], place[other], 0).astype(f32)
        for k in (1, 3, 2):
            block = pick(running[i], place[other] + k, 0)
            came = lax.ppermute(block, other, [(j, (j + k) % 4) for j in range(4)])
            total = total + came.astype(f32)
        sums.append(total)
    return sums


def body(patches, vit_gain, fc_in, fc_out, merge_gain, merge_shift, merger, counts, grad_packed):
    core = lax.axis_index("c")
    chip = lax.axis_index("x") * 4 + lax.axis_index("y")
    me = chip * 2 + core
    z = lax.axis_index("z")

    halves = merger.reshape(160, 2, 512)
    kept = lax.dynamic_index_in_dim(halves, core, 1, keepdims=False)
    given = lax.dynamic_index_in_dim(halves, 1 - core, 1, keepdims=False)
    got = lax.ppermute(given, "c", SWAP)
    both = jnp.where(core == 0, jnp.concatenate([kept, got]), jnp.concatenate([got, kept]))
    weight = lax.all_gather(both, ("x", "y"), axis=0, tiled=True)

    inputs = patches.astype(f32)
    normed = layer_norm(inputs, vit_gain, 0.0).astype(bf16)
    hidden = quick_gelu(jnp.dot(normed, fc_in, preferred_element_type=f32)).astype(bf16)
    summed = lax.psum_scatter(
        jnp.dot(hidden, fc_out, preferred_element_type=f32).astype(bf16),
        "z",
        scatter_dimension=0,
        tiled=True,
    ).astype(f32)

    slot = jnp.arange(16, dtype=jnp.int32)
    recv_counts = lax.dynamic_index_in_dim(counts, me, 1, keepdims=False)
    recv_start = exclusive_sum(recv_counts)
    packed_row = jnp.where(
        slot[None, :] < recv_counts[:, None], recv_start[:, None] + slot[None, :], -1
    ).reshape(512)
    pack = (packed_row[:, None] == jnp.arange(512, dtype=jnp.int32)[None, :]).astype(bf16)
    send_counts = lax.dynamic_slice_in_dim(counts, chip * 2, 2, 0)
    send_start = jnp.cumsum(send_counts, axis=1) - send_counts
    first = send_start.T[:, :, None] + slot + 256 * jnp.arange(2, dtype=jnp.int32)[None, :, None]
    token = jnp.where(slot < send_counts.T[:, :, None], first, -1).reshape(1024)
    route = (jnp.arange(512, dtype=jnp.int32)[:, None] == token[None, :]).astype(bf16)

    returning = jnp.stack(
        [
            jnp.dot(pack, grad_packed[:, :512], preferred_element_type=f32).astype(bf16).reshape(16, 32, 512),
            jnp.dot(pack, grad_packed[:, 512:], preferred_element_type=f32).astype(bf16).reshape(16, 32, 512),
        ],
        axis=1,
    ).reshape(32, 32, 512)
    arrived = lax.all_to_all(returning, DP, split_axis=0, concat_axis=0, tiled=True)
    token_grads = jnp.dot(
        route, arrived.reshape(1024, 512), preferred_element_type=f32
    ).astype(bf16)

    layer_out = lax.dynamic_slice_in_dim(inputs, z * 128, 128, 0) + summed
    average = jnp.mean(layer_out, axis=-1, keepdims=True)
    centered = layer_out - average
    inverse = lax.rsqrt(jnp.mean(centered * centered, axis=-1, keepdims=True) + epsilon)
    normal = centered * inverse
    normed_mine = (normal * merge_gain + merge_shift).astype(bf16)
    merged_own = lax.all_gather(normed_mine.reshape(32, 5120), "z", axis=0, tiled=True)
    merged_other = lax.ppermute(merged_own, "c", SWAP)
    merged = jnp.where(
        core == 0,
        jnp.concatenate([merged_own, merged_other]),
        jnp.concatenate([merged_other, merged_own]),
    )

    scale = 1.0 / math.sqrt(8192)
    parts = []
    for i, ax in enumerate("xy"):
        part = lax.dot_general(
            merged,
            token_grads[:, 256 * i : 256 * (i + 1)],
            (((0,), (0,)), ((), ())),
            preferred_element_type=f32,
        )
        parts.append((ax, (part * scale).astype(bf16).reshape(4, 4, 320, 256)))
    sums = scatter_chips(parts)
    chip_rows = jnp.concatenate(sums, axis=1).reshape(2, 160, 512)
    mine = lax.dynamic_index_in_dim(chip_rows, core, 0, keepdims=False)
    other = lax.ppermute(
        lax.dynamic_index_in_dim(chip_rows, 1 - core, 0, keepdims=False), "c", SWAP
    )
    grad_weight = jnp.where(
        core == 0,
        jnp.concatenate([mine, other], axis=1),
        jnp.concatenate([other, mine], axis=1),
    )

    projected = jnp.dot(merged, weight, preferred_element_type=f32).astype(bf16)
    outgoing = lax.dot_general(
        route, projected, (((0,), (0,)), ((), ())), preferred_element_type=f32
    ).astype(bf16)
    incoming = lax.all_to_all(
        outgoing.reshape(32, 32, 512), DP, split_axis=0, concat_axis=0, tiled=True
    ).reshape(16, 2, 512 // 16, 512)
    visual = jnp.concatenate(
        [
            lax.dot_general(
                pack,
                incoming[:, h].reshape(512, 512),
                (((0,), (0,)), ((), ())),
                preferred_element_type=f32,
            ).astype(bf16)
            for h in range(2)
        ],
        axis=1,
    )

    partial = lax.dot_general(
        token_grads, weight, (((1,), (1,)), ((), ())), preferred_element_type=f32
    ).astype(bf16).reshape(2, 256, 5120)
    kept = lax.dynamic_index_in_dim(partial, core, 0, keepdims=False)
    given = lax.dynamic_index_in_dim(partial, 1 - core, 0, keepdims=False)
    chip_grads = (kept.astype(f32) + lax.ppermute(given, "c", SWAP).astype(f32)).astype(bf16)
    merged_grads = (
        lax.psum_scatter(chip_grads, "z", scatter_dimension=0, tiled=True)
        .astype(f32)
        .reshape(128, 1280)
    )
    scaled = merged_grads * merge_gain
    grad_layer = inverse * (
        scaled
        - jnp.mean(scaled, axis=-1, keepdims=True)
        - normal * jnp.mean(scaled * normal, axis=-1, keepdims=True)
    )
    return (visual, grad_weight, grad_layer)


def solution(mesh):
    grid = Mesh(mesh.devices.reshape(4, 4, 2, 8), ("x", "y", "c", "z"))
    in_specs = (
        P(DP, None),
        P(),
        P(None, "z"),
        P("z", None),
        P(),
        P(),
        P(DP, "z"),
        P(),
        P(DP, "z"),
    )
    out_specs = (P(DP, "z"), P(DP, "z"), P((*DP, "z"), None))
    return jax.shard_map(body, mesh=grid, in_specs=in_specs, out_specs=out_specs, check_vma=False)
```

time: 312 us -> 293 us (0.939)
  other arithmetic: 61.2 us -> 27.3 us
  starting transfers between devices: 19.5 us -> 45.2 us
  waiting for transfers between devices: 163 us -> 155 us
  local copies, waits for them, and re-layouts: 15 us -> 9.66 us
    reduce_scatter x3 -> x2, waiting for transfers between devices: 89.7 us -> 33 us  [the longest x1 33 us: body(): lax.psum_scatter(chip_grads, 'z', scatter_dimension=0, tiled=True)]
    gather x10 -> x0, other arithmetic: 40.7 us -> none  [the longest x3 20.4 us: body(): recv_start[source]]
    ppermute x0 -> x16, starting transfers between devices: none -> 34.6 us  [the longest x6 14.2 us: scatter_chips(): came = lax.ppermute(running[i], DP, pairs[ax])]
    ppermute x0 -> x16, waiting for transfers between devices: none -> 33.8 us  [the longest x6 17 us: scatter_chips(): came = lax.ppermute(running[i], DP, pairs[ax])]
    gather x8 -> x0, local copies, waits for them, and re-layouts: 11.7 us -> none  [the longest x1 2.78 us: body(): grad_packed[back_rows]]
    convert_element_type x2 -> x8, other arithmetic: 6.37 us -> 16.3 us  [the longest x6 9.27 us: scatter_chips(): running[i] = (came.astype(f32) + mine.astype(f32)).astype(bf16)]
    all_to_all x2, starting transfers between devices: 19.1 us -> 10.4 us  [the longest x1 5.71 us: body(): lax.all_to_all(returning, DP, split_axis=0, concat_axis=0, tiled=True)]
    all_to_all x2, waiting for transfers between devices: 0.01 us -> 8.13 us  [the longest x1 8.13 us: body(): lax.all_to_all(returning, DP, split_axis=0, concat_axis=0, tiled=True)]
  transfers between devices with their start and end apart: 7 -> 22, of which waited for: 4 -> 12; matrix products, arithmetic and copies ran while one was open for 31% -> 20% of each run, Pallas kernels for 0% -> 0%
where the time goes in v1:
time: 293 us; the launch traced here: 292 us
  waiting for transfers between devices  155 us (53%)
  starting transfers between devices  45.2 us (15%)
  matrix products  38.8 us (13%)
  other arithmetic  27.3 us (9%)
  between operations  16 us (5%)
  local copies, waits for them, and re-layouts  9.66 us (3%)
    all_gather x1, waiting for transfers between devices, body(): lax.all_gather(normed_mine.reshape(32, 5120), 'z', axis=0, tiled=True)  43.2 us
    all_gather x1, waiting for transfers between devices, body(): weight = lax.all_gather(both, ('x', 'y'), axis=0, tiled=True)  37 us
    reduce_scatter x1, waiting for transfers between devices, body(): lax.psum_scatter(chip_grads, 'z', scatter_dimension=0, tiled=True)  33 us
    ppermute x6, waiting for transfers between devices, scatter_chips(): came = lax.ppermute(running[i], DP, pairs[ax])  17 us
    ppermute x6, starting transfers between devices, scatter_chips(): came = lax.ppermute(running[i], DP, pairs[ax])  14.2 us
    dot_general x1, matrix products, body(): lax.dot_general(route, projected, (((0,), (0,)), ((), ())), preferred_ele...  10.1 us
    dot_general x2, matrix products, body(): lax.dot_general(merged, token_grads[:, 256 * i:256 * (i + 1)], (((0,), (0...  9.96 us
    convert_element_type x6, other arithmetic, scatter_chips(): running[i] = (came.astype(f32) + mine.astype(f32)).astype(bf16)  9.27 us
  transfers between devices with their start and end apart: 22, of which 12 were waited for; matrix products, arithmetic and copies ran while one was open for 20% of the time, Pallas kernels for 0%

profile of v1, /device:TPU:1, one launch (start us, length us, event | category | flops | bytes accessed | tf_op | source)
XLA Modules:
  0.0 292.2 jit_solution(7249101876729904777)
XLA Ops:
  10.1 3.3 %collective-permute-start.1 = (bf16[160,512]{1,0:T(8,128)(2,1)S(1)}, bf16[160,512]{1,0:T(8,128)(2,1)S(1)}, u32[]{:S(2)}, u32[]{:S(2)}) collective-permute-start(bf16[160,512]{1,0:T(8,128)(2,1)S(1)} %bitcast.107), channel_id=1, source_target_pairs={{0,8},{8,0},{1,9},{9,1},{2,10},{10,2},{3,11},{11,3},{4,12},{12,4},... | collective-permute-start | bytes 491528 | tf_op jit(solution)/shard_map/ppermute | solution.py:82
  20.0 5.7 %all-to-all-start.1 = ((bf16[32,32,512]{2,1,0:T(8,128)(2,1)}), bf16[32,32,512]{2,1,0:T(8,128)(2,1)S(1)}, u32[]{:S(2)}, u32[]{:S(2)}) async-start(bf16[32,32,512]{2,1,0:T(8,128)(2,1)} %bitcast.10), calls=%async_computation.2 | async-start | bytes 2097152 | tf_op jit(solution)/shard_map/all_to_all | solution.py:116
  29.1 8.3 %convolution_convert_fusion.1 = bf16[1024,1280]{1,0:T(8,128)(2,1)} fusion(bf16[640,1280]{1,0:T(8,128)(2,1)S(1)} %copy-done, bf16[1280,640]{1,0:T(8,128)(2,1)} %param.11, bf16[1024,1280]{1,0:T(8,128)(2,1)} %param.9, f32[1280]{0:T(1024)S(1)} %copy-done.9, f32[1024]{0:T(1024)S(1)} %add_rsqrt_fusion, f32[1024]{0:T(1024)S(1)} %broadcast_multiply_fusion), kind=kOutput, calls=%fused_computation.11 | convolution fusion | flops 3367239680 | bytes 8532992 | tf_op jit(solution)/shard_map/dot_general | solution.py:90
  38.2 8.1 %all-to-all-done.1 = bf16[32,32,512]{2,1,0:T(8,128)(2,1)S(1)} async-done(((bf16[32,32,512]{2,1,0:T(8,128)(2,1)}), bf16[32,32,512]{2,1,0:T(8,128)(2,1)S(1)}, u32[]{:S(2)}, u32[]{:S(2)}) %all-to-all-start.1) | async-done | bytes 1048608 | tf_op jit(solution)/shard_map/all_to_all | solution.py:116
  47.0 37.0 %all-gather.5.cloned.1.call-done = bf16[5120,512]{1,0:T(8,128)(2,1)} async-done(((bf16[320,512]{1,0:T(8,128)(2,1)}), bf16[5120,512]{1,0:T(8,128)(2,1)}) %all-gather.5.cloned.1.call-update) | async-done | bytes 5242896 | tf_op jit(solution)/shard_map/all_gather | solution.py:84
  84.0 5.6 %convolution_convert_fusion = bf16[512,5120]{1,0:T(8,128)(2,1)S(1)} fusion(bf16[512,512]{1,0:T(8,128)(2,1)S(1)} %fusion.18, bf16[5120,512]{1,0:T(8,128)(2,1)} %all-gather.5.cloned.1.call-done), kind=kOutput, calls=%fused_computation | convolution fusion | flops 2686976000 | bytes 11010048 | tf_op jit(solution)/shard_map/dot_general | solution.py:177
  90.8 4.5 %collective-permute-done.15 = bf16[256,5120]{1,0:T(8,128)(2,1)S(1)} collective-permute-done((bf16[256,5120]{1,0:T(8,128)(2,1)S(1)}, bf16[256,5120]{1,0:T(8,128)(2,1)S(1)}, u32[]{:S(2)}, u32[]{:S(2)}) %collective-permute-start.15) | collective-permute-done | bytes 2621472 | tf_op jit(solution)/shard_map/ppermute | solution.py:182
  95.4 2.6 fusion.2
  98.0 4.5 %convert_element_type.165 = f32[1024,1280]{1,0:T(8,128)} convert(bf16[1024,1280]{1,0:T(8,128)(2,1)} %param.9) | non-fusion elementwise | flops 1310720 | bytes 7864320 | tf_op jit(solution)/shard_map/convert_element_type | solution.py:86
  104.1 33.0 %reduce-scatter.5.cloned.1.call-done = bf16[32,5120]{1,0:T(8,128)(2,1)} async-done(((bf16[256,5120]{1,0:T(8,128)(2,1)}), bf16[32,5120]{1,0:T(8,128)(2,1)}) %reduce-scatter.5.cloned.1.call-update) | async-done | bytes 327696 | tf_op jit(solution)/shard_map/reduce_scatter | solution.py:184
  140.6 43.2 %all-gather.3.cloned.1.call-done = bf16[256,5120]{1,0:T(8,128)(2,1)} async-done(((bf16[32,5120]{1,0:T(8,128)(2,1)}), bf16[256,5120]{1,0:T(8,128)(2,1)}) %all-gather.3.cloned.1.call-update) | async-done | bytes 2621456 | tf_op jit(solution)/shard_map/all_gather | solution.py:127
  183.8 3.6 %collective-permute-start = (bf16[256,5120]{1,0:T(8,128)(2,1)}, bf16[256,5120]{1,0:T(8,128)(2,1)}, u32[]{:S(2)}, u32[]{:S(2)}) collective-permute-start(bf16[256,5120]{1,0:T(8,128)(2,1)} %all-gather.3.cloned.1.call-done), channel_id=1, source_target_pairs={{0,8},{8,0},{1,9},{9,1},{2,10},{10,2},{3,11},{11,3},{4,12},{12,4},... | collective-permute-start | bytes 7864328 | tf_op jit(solution)/shard_map/ppermute | solution.py:128
  187.4 4.9 %collective-permute-done = bf16[256,5120]{1,0:T(8,128)(2,1)} collective-permute-done((bf16[256,5120]{1,0:T(8,128)(2,1)}, bf16[256,5120]{1,0:T(8,128)(2,1)}, u32[]{:S(2)}, u32[]{:S(2)}) %collective-permute-start) | collective-permute-done | bytes 2621472 | tf_op jit(solution)/shard_map/ppermute | solution.py:128
  192.3 5.5 %fusion = bf16[5120,256]{1,0:T(8,128)(2,1)S(1)} fusion(bf16[512,512]{1,0:T(8,128)(2,1)S(1)} %copy-done.11, bf16[256,5120]{1,0:T(8,128)(2,1)} %collective-permute-done, bf16[256,5120]{1,0:T(8,128)(2,1)} %all-gather.3.cloned.1.call-done, pred[]{:T(512)S(6)} %eq.54), kind=kOutput, calls=%fused_computation.3 | convolution fusion | flops 1368391680 | bytes 8126465 | tf_op jit(solution)/shard_map/dot_general | solution.py:138
  201.9 4.4 %fusion.1 = bf16[5120,256]{1,0:T(8,128)(2,1)S(1)} fusion(bf16[512,512]{1,0:T(8,128)(2,1)S(1)} %copy-done.11, bf16[256,5120]{1,0:T(8,128)(2,1)} %collective-permute-done, bf16[256,5120]{1,0:T(8,128)(2,1)S(1)} %copy-done.8, pred[]{:T(512)S(6)} %eq.54), kind=kOutput, calls=%fused_computation.4 | convolution fusion | flops 1368391680 | bytes 8126465 | tf_op jit(solution)/shard_map/dot_general | solution.py:138
  207.8 2.5 collective-permute-start.8
  210.4 10.1 %fusion.9 = bf16[1024,512]{1,0:T(8,128)(2,1)} fusion(s32[1024]{0:T(1024)S(1)} %select_n.192, bf16[5120,512]{1,0:T(8,128)(2,1)} %all-gather.5.cloned.1.call-done, bf16[256,5120]{1,0:T(8,128)(2,1)} %collective-permute-done, bf16[256,5120]{1,0:T(8,128)(2,1)} %all-gather.3.cloned.1.call-done, pred[]{:T(512)S(6)} %eq.54), kind=kOutput, calls=%fused_computation.21 | convolution fusion | flops 3246129152 | bytes 11538433 | tf_op jit(solution)/shard_map/dot_general | solution.py:158
  220.5 4.7 %all-to-all-start = ((bf16[32,32,512]{2,1,0:T(8,128)(2,1)}), bf16[32,32,512]{2,1,0:T(8,128)(2,1)S(1)}, u32[]{:S(2)}, u32[]{:S(2)}) async-start(bf16[32,32,512]{2,1,0:T(8,128)(2,1)} %bitcast.2), calls=%async_computation.1 | async-start | bytes 2097152 | tf_op jit(solution)/shard_map/all_to_all | solution.py:161
  226.7 2.7 collective-permute-start.3
  230.8 2.7 collective-permute-start.9
  233.6 12.7 %collective-permute-done.3 = bf16[4,320,256]{2,1,0:T(8,128)(2,1)} collective-permute-done((bf16[4,320,256]{2,1,0:T(8,128)(2,1)S(1)}, bf16[4,320,256]{2,1,0:T(8,128)(2,1)}, u32[]{:S(2)}, u32[]{:S(2)}) %collective-permute-start.3) | collective-permute-done | bytes 655392 | tf_op jit(solution)/shard_map/ppermute | solution.py:58
  254.3 4.3 %collective-permute-done.4 = bf16[4,320,256]{2,1,0:T(8,128)(2,1)} collective-permute-done((bf16[4,320,256]{2,1,0:T(8,128)(2,1)}, bf16[4,320,256]{2,1,0:T(8,128)(2,1)}, u32[]{:S(2)}, u32[]{:S(2)}) %collective-permute-start.4) | collective-permute-done | bytes 655392 | tf_op jit(solution)/shard_map/ppermute | solution.py:58
  272.4 3.4 %collective-permute-done.13 = bf16[320,256]{1,0:T(8,128)(2,1)S(1)} collective-permute-done((bf16[320,256]{1,0:T(8,128)(2,1)S(1)}, bf16[320,256]{1,0:T(8,128)(2,1)S(1)}, u32[]{:S(2)}, u32[]{:S(2)}) %collective-permute-start.13) | collective-permute-done | bytes 163872 | tf_op jit(solution)/shard_map/ppermute | solution.py:67
  276.0 4.6 %collective-permute-start.14 = (f32[160,512]{1,0:T(8,128)S(1)}, f32[160,512]{1,0:T(8,128)}, u32[]{:S(2)}, u32[]{:S(2)}) collective-permute-start(f32[160,512]{1,0:T(8,128)S(1)} %get-tuple-element.23), channel_id=1, source_target_pairs={{0,8},{8,0},{1,9},{9,1},{2,10},{10,2},{3,11},{11,3},{4,12},{12,4},... | collective-permute-start | bytes 983048 | tf_op jit(solution)/shard_map/ppermute | solution.py:148
  (112 shorter events, 54.0 us)
Async XLA Ops:
  8.0 76.0 %all-gather.5.cloned.1.call-start = ((), (), s32[]{:S(2)}) async-start(), calls=%async_computation.6 | async-start | bytes 5570560 | tf_op jit(solution)/shard_map/all_gather | solution.py:84
  10.1 4.4 %collective-permute-start.1 = (bf16[160,512]{1,0:T(8,128)(2,1)S(1)}, bf16[160,512]{1,0:T(8,128)(2,1)S(1)}, u32[]{:S(2)}, u32[]{:S(2)}) collective-permute-start(bf16[160,512]{1,0:T(8,128)(2,1)S(1)} %bitcast.107), channel_id=1, source_target_pairs={{0,8},{8,0},{1,9},{9,1},{2,10},{10,2},{3,11},{11,3},{4,12},{12,4},... | collective-permute-start | bytes 491528 | tf_op jit(solution)/shard_map/ppermute | solution.py:82
  20.0 26.3 %all-to-all-start.1 = ((bf16[32,32,512]{2,1,0:T(8,128)(2,1)}), bf16[32,32,512]{2,1,0:T(8,128)(2,1)S(1)}, u32[]{:S(2)}, u32[]{:S(2)}) async-start(bf16[32,32,512]{2,1,0:T(8,128)(2,1)} %bitcast.10), calls=%async_computation.2 | async-start | bytes 2097152 | tf_op jit(solution)/shard_map/all_to_all | solution.py:116
  25.7 76.8 %reduce-scatter.3.cloned.1.call-start = ((), (), s32[]{:S(2)}) async-start(), calls=%async_computation.4 | async-start | bytes 2949120 | tf_op jit(solution)/shard_map/reduce_scatter | solution.py:89
  37.4 99.7 %reduce-scatter.5.cloned.1.call-start = ((), (), s32[]{:S(2)}) async-start(), calls=%async_computation.7 | async-start | bytes 2949120 | tf_op jit(solution)/shard_map/reduce_scatter | solution.py:184
  47.0 42.7 %copy-start.10 = (bf16[512,512]{1,0:T(8,128)(2,1)}, bf16[512,512]{1,0:T(8,128)(2,1)S(1)}, u32[]{:S(2)}) copy-start(bf16[512,512]{1,0:T(8,128)(2,1)S(1)} %fusion.18) | copy-start | bytes 1572868
  89.9 5.5 %collective-permute-start.15 = (bf16[256,5120]{1,0:T(8,128)(2,1)S(1)}, bf16[256,5120]{1,0:T(8,128)(2,1)S(1)}, u32[]{:S(2)}, u32[]{:S(2)}) collective-permute-start(bf16[256,5120]{1,0:T(8,128)(2,1)S(1)} %dynamic-slice_bitcast_fusion), channel_id=1, source_target_pairs={{0,8},{8,0},{1,9},{9,1},{2,10},{10,2},{3,11},{11,3},{4,12},{12,4},... | collective-permute-start | bytes 7864328 | tf_op jit(solution)/shard_map/ppermute | solution.py:182
  98.0 85.8 %all-gather.3.cloned.1.call-start = ((), (), s32[]{:S(2)}) async-start(), calls=%async_computation.5 | async-start | bytes 2949120 | tf_op jit(solution)/shard_map/all_gather | solution.py:127
  138.3 54.0 %copy-start.11 = (bf16[512,512]{1,0:T(8,128)(2,1)S(1)}, bf16[512,512]{1,0:T(8,128)(2,1)}, u32[]{:S(2)}) copy-start(bf16[512,512]{1,0:T(8,128)(2,1)} %copy-done.10) | copy-start | bytes 1572868
  183.8 8.5 %collective-permute-start = (bf16[256,5120]{1,0:T(8,128)(2,1)}, bf16[256,5120]{1,0:T(8,128)(2,1)}, u32[]{:S(2)}, u32[]{:S(2)}) collective-permute-start(bf16[256,5120]{1,0:T(8,128)(2,1)} %all-gather.3.cloned.1.call-done), channel_id=1, source_target_pairs={{0,8},{8,0},{1,9},{9,1},{2,10},{10,2},{3,11},{11,3},{4,12},{12,4},... | collective-permute-start | bytes 7864328 | tf_op jit(solution)/shard_map/ppermute | solution.py:128
  199.4 25.8 %collective-permute-start.2 = (bf16[4,320,256]{2,1,0:T(8,128)(2,1)S(1)}, bf16[4,320,256]{2,1,0:T(8,128)(2,1)}, u32[]{:S(2)}, u32[]{:S(2)}) collective-permute-start(bf16[4,320,256]{2,1,0:T(8,128)(2,1)S(1)} %dynamic-slice_bitcast_fusion.2), channel_id=1, source_target_pairs={{0,64},{8,200},{16,80},{24,216},{32,96},{40,232},{48,112},{56,248}... | collective-permute-start | bytes 1966088 | tf_op jit(solution)/shard_map/ppermute | solution.py:58
  207.8 21.5 %collective-permute-start.8 = (bf16[4,320,256]{2,1,0:T(8,128)(2,1)S(1)}, bf16[4,320,256]{2,1,0:T(8,128)(2,1)}, u32[]{:S(2)}, u32[]{:S(2)}) collective-permute-start(bf16[4,320,256]{2,1,0:T(8,128)(2,1)S(1)} %dynamic-slice_bitcast_fusion.1), channel_id=1, source_target_pairs={{0,16},{8,56},{16,32},{24,8},{32,48},{40,24},{48,0},{56,40},{64,80... | collective-permute-start | bytes 1966088 | tf_op jit(solution)/shard_map/ppermute | solution.py:58
  220.5 33.2 %all-to-all-start = ((bf16[32,32,512]{2,1,0:T(8,128)(2,1)}), bf16[32,32,512]{2,1,0:T(8,128)(2,1)S(1)}, u32[]{:S(2)}, u32[]{:S(2)}) async-start(bf16[32,32,512]{2,1,0:T(8,128)(2,1)} %bitcast.2), calls=%async_computation.1 | async-start | bytes 2097152 | tf_op jit(solution)/shard_map/all_to_all | solution.py:161
  226.7 19.6 %collective-permute-start.3 = (bf16[4,320,256]{2,1,0:T(8,128)(2,1)S(1)}, bf16[4,320,256]{2,1,0:T(8,128)(2,1)}, u32[]{:S(2)}, u32[]{:S(2)}) collective-permute-start(bf16[4,320,256]{2,1,0:T(8,128)(2,1)S(1)} %fusion.15), channel_id=1, source_target_pairs={{0,64},{8,200},{16,80},{24,216},{32,96},{40,232},{48,112},{56,248}... | collective-permute-start | bytes 1966088 | tf_op jit(solution)/shard_map/ppermute | solution.py:58
  230.8 19.0 %collective-permute-start.9 = (bf16[4,320,256]{2,1,0:T(8,128)(2,1)S(1)}, bf16[4,320,256]{2,1,0:T(8,128)(2,1)}, u32[]{:S(2)}, u32[]{:S(2)}) collective-permute-start(bf16[4,320,256]{2,1,0:T(8,128)(2,1)S(1)} %fusion.12), channel_id=1, source_target_pairs={{0,16},{8,56},{16,32},{24,8},{32,48},{40,24},{48,0},{56,40},{64,80... | collective-permute-start | bytes 1966088 | tf_op jit(solution)/shard_map/ppermute | solution.py:58
  248.6 10.0 %collective-permute-start.4 = (bf16[4,320,256]{2,1,0:T(8,128)(2,1)}, bf16[4,320,256]{2,1,0:T(8,128)(2,1)}, u32[]{:S(2)}, u32[]{:S(2)}) collective-permute-start(bf16[4,320,256]{2,1,0:T(8,128)(2,1)} %fusion.14), channel_id=1, source_target_pairs={{0,64},{8,200},{16,80},{24,216},{32,96},{40,232},{48,112},{56,248}... | collective-permute-start | bytes 1966088 | tf_op jit(solution)/shard_map/ppermute | solution.py:58
  251.3 13.0 %collective-permute-start.10 = (bf16[4,320,256]{2,1,0:T(8,128)(2,1)S(1)}, bf16[4,320,256]{2,1,0:T(8,128)(2,1)S(1)}, u32[]{:S(2)}, u32[]{:S(2)}) collective-permute-start(bf16[4,320,256]{2,1,0:T(8,128)(2,1)S(1)} %fusion.11), channel_id=1, source_target_pairs={{0,16},{8,56},{16,32},{24,8},{32,48},{40,24},{48,0},{56,40},{64,80... | collective-permute-start | bytes 1966088 | tf_op jit(solution)/shard_map/ppermute | solution.py:58
  260.1 8.3 %collective-permute-start.5 = (bf16[320,256]{1,0:T(8,128)(2,1)S(1)}, bf16[320,256]{1,0:T(8,128)(2,1)S(1)}, u32[]{:S(2)}, u32[]{:S(2)}) collective-permute-start(bf16[320,256]{1,0:T(8,128)(2,1)S(1)} %get-tuple-element.24), channel_id=1, source_target_pairs={{0,16},{16,32},{32,48},{48,0},{1,17},{17,33},{33,49},{49,1},{2,18}... | collective-permute-start | bytes 491528 | tf_op jit(solution)/shard_map/ppermute | solution.py:67
  261.4 8.0 %collective-permute-start.6 = (bf16[320,256]{1,0:T(8,128)(2,1)S(1)}, bf16[320,256]{1,0:T(8,128)(2,1)S(1)}, u32[]{:S(2)}, u32[]{:S(2)}) collective-permute-start(bf16[320,256]{1,0:T(8,128)(2,1)S(1)} %get-tuple-element.26), channel_id=1, source_target_pairs={{0,48},{16,0},{32,16},{48,32},{1,49},{17,1},{33,17},{49,33},{2,50}... | collective-permute-start | bytes 491528 | tf_op jit(solution)/shard_map/ppermute | solution.py:67
  262.9 6.5 %collective-permute-start.7 = (bf16[320,256]{1,0:T(8,128)(2,1)S(1)}, bf16[320,256]{1,0:T(8,128)(2,1)S(1)}, u32[]{:S(2)}, u32[]{:S(2)}) collective-permute-start(bf16[320,256]{1,0:T(8,128)(2,1)S(1)} %get-tuple-element.25), channel_id=1, source_target_pairs={{0,32},{16,48},{32,0},{48,16},{1,33},{17,49},{33,1},{49,17},{2,34}... | collective-permute-start | bytes 491528 | tf_op jit(solution)/shard_map/ppermute | solution.py:67
  265.6 5.5 %collective-permute-start.11 = (bf16[320,256]{1,0:T(8,128)(2,1)S(1)}, bf16[320,256]{1,0:T(8,128)(2,1)S(1)}, u32[]{:S(2)}, u32[]{:S(2)}) collective-permute-start(bf16[320,256]{1,0:T(8,128)(2,1)S(1)} %get-tuple-element.27), channel_id=1, source_target_pairs={{0,64},{64,128},{128,192},{192,0},{1,65},{65,129},{129,193},{193,1... | collective-permute-start | bytes 491528 | tf_op jit(solution)/shard_map/ppermute | solution.py:67
  266.6 5.8 %collective-permute-start.12 = (bf16[320,256]{1,0:T(8,128)(2,1)S(1)}, bf16[320,256]{1,0:T(8,128)(2,1)S(1)}, u32[]{:S(2)}, u32[]{:S(2)}) collective-permute-start(bf16[320,256]{1,0:T(8,128)(2,1)S(1)} %get-tuple-element.29), channel_id=1, source_target_pairs={{0,192},{64,0},{128,64},{192,128},{1,193},{65,1},{129,65},{193,129... | collective-permute-start | bytes 491528 | tf_op jit(solution)/shard_map/ppermute | solution.py:67
  268.4 7.4 %collective-permute-start.13 = (bf16[320,256]{1,0:T(8,128)(2,1)S(1)}, bf16[320,256]{1,0:T(8,128)(2,1)S(1)}, u32[]{:S(2)}, u32[]{:S(2)}) collective-permute-start(bf16[320,256]{1,0:T(8,128)(2,1)S(1)} %get-tuple-element.28), channel_id=1, source_target_pairs={{0,128},{64,192},{128,0},{192,64},{1,129},{65,193},{129,1},{193,65... | collective-permute-start | bytes 491528 | tf_op jit(solution)/shard_map/ppermute | solution.py:67
  276.0 6.6 %collective-permute-start.14 = (f32[160,512]{1,0:T(8,128)S(1)}, f32[160,512]{1,0:T(8,128)}, u32[]{:S(2)}, u32[]{:S(2)}) collective-permute-start(f32[160,512]{1,0:T(8,128)S(1)} %get-tuple-element.23), channel_id=1, source_target_pairs={{0,8},{8,0},{1,9},{9,1},{2,10},{10,2},{3,11},{11,3},{4,12},{12,4},... | collective-permute-start | bytes 983048 | tf_op jit(solution)/shard_map/ppermute | solution.py:148
  (10 other events, 127.8 us)
Sparse Core Ops, SparseCore 0:
  15.5 68.5 all-gather.4
Sparse Core Ops, SparseCore 1:
  37.5 42.6 reduce-scatter.2
  98.0 39.0 reduce-scatter.4
  140.7 43.0 all-gather.2

commit v2 on v1

--- a/solution.py
+++ b/solution.py
@@ -102,7 +102,8 @@
     pack = (packed_row[:, None] == jnp.arange(512, dtype=jnp.int32)[None, :]).astype(bf16)
     send_counts = lax.dynamic_slice_in_dim(counts, chip * 2, 2, 0)
     send_start = jnp.cumsum(send_counts, axis=1) - send_counts
-    first = send_start.T[:, :, None] + slot + 256 * jnp.arange(2, dtype=jnp.int32)[None, :, None]
+    base = 256 * (jnp.arange(2, dtype=jnp.int32) ^ core)
+    first = send_start.T[:, :, None] + slot + base[None, :, None]
     token = jnp.where(slot < send_counts.T[:, :, None], first, -1).reshape(1024)
     route = (jnp.arange(512, dtype=jnp.int32)[:, None] == token[None, :]).astype(bf16)
 
@@ -126,11 +127,7 @@
     normed_mine = (normal * merge_gain + merge_shift).astype(bf16)
     merged_own = lax.all_gather(normed_mine.reshape(32, 5120), "z", axis=0, tiled=True)
     merged_other = lax.ppermute(merged_own, "c", SWAP)
-    merged = jnp.where(
-        core == 0,
-        jnp.concatenate([merged_own, merged_other]),
-        jnp.concatenate([merged_other, merged_own]),
-    )
+    merged = jnp.concatenate([merged_own, merged_other])
 
     scale = 1.0 / math.sqrt(8192)
     parts = []
@@ -174,12 +171,13 @@
         axis=1,
     )
 
+    held_grads, _ = lax.optimization_barrier((token_grads, normed_mine))
     partial = lax.dot_general(
-        token_grads, weight, (((1,), (1,)), ((), ())), preferred_element_type=f32
-    ).astype(bf16).reshape(2, 256, 5120)
-    kept = lax.dynamic_index_in_dim(partial, core, 0, keepdims=False)
-    given = lax.dynamic_index_in_dim(partial, 1 - core, 0, keepdims=False)
-    chip_grads = (kept.astype(f32) + lax.ppermute(given, "c", SWAP).astype(f32)).astype(bf16)
+        held_grads, weight, (((1,), (1,)), ((), ())), preferred_element_type=f32
+    ).astype(bf16)
+    chip_grads = (
+        partial[:256].astype(f32) + lax.ppermute(partial[256:], "c", SWAP).astype(f32)
+    ).astype(bf16)
     merged_grads = (
         lax.psum_scatter(chip_grads, "z", scatter_dimension=0, tiled=True)
         .astype(f32)

time: 293 us -> 283 us (0.966)
  waiting for transfers between devices: 155 us -> 145 us
  matrix products: 38.8 us -> 31.8 us
  local copies, waits for them, and re-layouts: 9.66 us -> 14.4 us
    reduce_scatter x1, waiting for transfers between devices: 0.01 us -> 39.4 us  [body(): lax.psum_scatter(jnp.dot(hidden, fc_out, preferred_element_type=f32).asty...]
    reduce_scatter x1, waiting for transfers between devices: 33 us -> 0.01 us  [body(): lax.psum_scatter(chip_grads, 'z', scatter_dimension=0, tiled=True)]
    all_gather x1, waiting for transfers between devices: 37 us -> 61.1 us  [body(): weight = lax.all_gather(both, ('x', 'y'), axis=0, tiled=True)]
    all_gather x1, waiting for transfers between devices: 43.2 us -> 23.3 us  [body(): lax.all_gather(normed_mine.reshape(32, 5120), 'z', axis=0, tiled=True)]
    all_to_all x1, waiting for transfers between devices: 8.13 us -> 0.01 us  [body(): lax.all_to_all(returning, DP, split_axis=0, concat_axis=0, tiled=True)]
    dot_general x2, matrix products: 9.96 us -> 4.67 us  [body(): lax.dot_general(merged, token_grads[:, 256 * i:256 * (i + 1)], (((0,), (0...]
    ppermute x1, waiting for transfers between devices: 4.88 us -> 0.01 us  [body(): merged_other = lax.ppermute(merged_own, 'c', SWAP)]
    ppermute x1, waiting for transfers between devices: 4.54 us -> 0.01 us  [body(): lax.ppermute(partial[256:], 'c', SWAP).astype(f32)]
  transfers between devices with their start and end apart: 22 -> 22, of which waited for: 12 -> 9; matrix products, arithmetic and copies ran while one was open for 20% -> 21% of each run, Pallas kernels for 0% -> 0%
where the time goes in v2:
time: 283 us; the launch traced here: 282 us
  waiting for transfers between devices  145 us (51%)
  starting transfers between devices  46.1 us (16%)
  matrix products  31.8 us (11%)
  other arithmetic  29.8 us (11%)
  local copies, waits for them, and re-layouts  14.4 us (5%)
  between operations  14.2 us (5%)
    all_gather x1, waiting for transfers between devices, body(): weight = lax.all_gather(both, ('x', 'y'), axis=0, tiled=True)  61.1 us
    reduce_scatter x1, waiting for transfers between devices, body(): lax.psum_scatter(jnp.dot(hidden, fc_out, preferred_element_type=f32).asty...  39.4 us
    all_gather x1, waiting for transfers between devices, body(): lax.all_gather(normed_mine.reshape(32, 5120), 'z', axis=0, tiled=True)  23.3 us
    ppermute x6, waiting for transfers between devices, scatter_chips(): came = lax.ppermute(running[i], DP, pairs[ax])  15.7 us
    ppermute x6, starting transfers between devices, scatter_chips(): came = lax.ppermute(running[i], DP, pairs[ax])  12.1 us
    convert_element_type x6, other arithmetic, scatter_chips(): running[i] = (came.astype(f32) + mine.astype(f32)).astype(bf16)  11 us
    dot_general x1, matrix products, body(): lax.dot_general(route, projected, (((0,), (0,)), ((), ())), preferred_ele...  8.52 us
    ppermute x6, starting transfers between devices, scatter_chips(): came = lax.ppermute(block, other, [(j, (j + k) % 4) for j in range(4)])  8.18 us
  transfers between devices with their start and end apart: 22, of which 9 were waited for; matrix products, arithmetic and copies ran while one was open for 21% of the time, Pallas kernels for 0%

profile of v2, /device:TPU:1, one launch (start us, length us, event | category | flops | bytes accessed | tf_op | source)
XLA Modules:
  0.0 281.8 jit_solution(2514551070364191464)
XLA Ops:
  7.2 2.3 convert_reduce_fusion
  10.7 8.1 %convolution_convert_fusion.1 = bf16[1024,1280]{1,0:T(8,128)(2,1)} fusion(bf16[640,1280]{1,0:T(8,128)(2,1)S(1)} %copy-done, bf16[1280,640]{1,0:T(8,128)(2,1)} %param.11, bf16[1024,1280]{1,0:T(8,128)(2,1)} %param.9, f32[1280]{0:T(1024)S(1)} %copy-done.10, f32[1024]{0:T(1024)S(1)} %add_rsqrt_fusion, f32[1024]{0:T(1024)S(1)} %broadcast_multiply_fusion), kind=kOutput, calls=%fused_computation.9 | convolution fusion | flops 3367239680 | bytes 8532992 | tf_op jit(solution)/shard_map/dot_general | solution.py:90
  19.0 4.5 %convert_element_type.162 = f32[1024,1280]{1,0:T(8,128)} convert(bf16[1024,1280]{1,0:T(8,128)(2,1)} %param.9) | non-fusion elementwise | flops 1310720 | bytes 7864320 | tf_op jit(solution)/shard_map/convert_element_type | solution.py:86
  23.4 39.4 %reduce-scatter.3.cloned.1.call-done = bf16[128,1280]{1,0:T(8,128)(2,1)} async-done(((bf16[1024,1280]{1,0:T(8,128)(2,1)}), bf16[128,1280]{1,0:T(8,128)(2,1)}) %reduce-scatter.3.cloned.1.call-update) | async-done | bytes 327696 | tf_op jit(solution)/shard_map/reduce_scatter | solution.py:89
  66.6 4.9 %collective-permute-start.1 = (bf16[160,512]{1,0:T(8,128)(2,1)S(1)}, bf16[160,512]{1,0:T(8,128)(2,1)S(1)}, u32[]{:S(2)}, u32[]{:S(2)}) collective-permute-start(bf16[160,512]{1,0:T(8,128)(2,1)S(1)} %bitcast.104), channel_id=1, source_target_pairs={{0,8},{8,0},{1,9},{9,1},{2,10},{10,2},{3,11},{11,3},{4,12},{12,4},... | collective-permute-start | bytes 491528 | tf_op jit(solution)/shard_map/ppermute | solution.py:82
  78.0 7.2 %all-to-all-start.1 = ((bf16[32,32,512]{2,1,0:T(8,128)(2,1)}), bf16[32,32,512]{2,1,0:T(8,128)(2,1)S(1)}, u32[]{:S(2)}, u32[]{:S(2)}) async-start(bf16[32,32,512]{2,1,0:T(8,128)(2,1)} %bitcast.10), calls=%async_computation.2 | async-start | bytes 2097152 | tf_op jit(solution)/shard_map/all_to_all | solution.py:117
  85.3 23.3 %all-gather.3.cloned.1.call-done = bf16[256,5120]{1,0:T(8,128)(2,1)} async-done(((bf16[32,5120]{1,0:T(8,128)(2,1)}), bf16[256,5120]{1,0:T(8,128)(2,1)}) %all-gather.3.cloned.1.call-update) | async-done | bytes 2621456 | tf_op jit(solution)/shard_map/all_gather | solution.py:128
  108.6 3.6 %collective-permute-start = (bf16[256,5120]{1,0:T(8,128)(2,1)}, bf16[256,5120]{1,0:T(8,128)(2,1)}, u32[]{:S(2)}, u32[]{:S(2)}) collective-permute-start(bf16[256,5120]{1,0:T(8,128)(2,1)} %all-gather.3.cloned.1.call-done), channel_id=1, source_target_pairs={{0,8},{8,0},{1,9},{9,1},{2,10},{10,2},{3,11},{11,3},{4,12},{12,4},... | collective-permute-start | bytes 7864328 | tf_op jit(solution)/shard_map/ppermute | solution.py:129
  113.6 61.1 %all-gather.5.cloned.1.call-done = bf16[5120,512]{1,0:T(8,128)(2,1)} async-done(((bf16[320,512]{1,0:T(8,128)(2,1)}), bf16[5120,512]{1,0:T(8,128)(2,1)}) %all-gather.5.cloned.1.call-update) | async-done | bytes 5242896 | tf_op jit(solution)/shard_map/all_gather | solution.py:84
  174.6 5.6 %convolution_convert_fusion = bf16[512,5120]{1,0:T(8,128)(2,1)S(1)} fusion(bf16[512,512]{1,0:T(8,128)(2,1)S(1)} %fusion.17, bf16[5120,512]{1,0:T(8,128)(2,1)} %all-gather.5.cloned.1.call-done), kind=kOutput, calls=%fused_computation | convolution fusion | flops 2686976000 | bytes 11010048 | tf_op jit(solution)/shard_map/dot_general | solution.py:175
  189.6 2.5 collective-permute-start.8
  192.1 3.1 %fusion = bf16[5120,256]{1,0:T(8,128)(2,1)} fusion(bf16[512,5120]{1,0:T(8,128)(2,1)S(1)} %constant_dynamic-update-slice_fusion, bf16[512,512]{1,0:T(8,128)(2,1)S(1)} %fusion.17), kind=kOutput, calls=%fused_computation.3 | convolution fusion | flops 1344798720 | bytes 8126464 | tf_op jit(solution)/shard_map/dot_general | solution.py:135
  195.2 4.3 %add_convert_fusion = bf16[256,5120]{1,0:T(8,128)(2,1)} fusion(bf16[256,5120]{1,0:T(8,128)(2,1)} %collective-permute-done.15, bf16[512,5120]{1,0:T(8,128)(2,1)S(1)} %bitcast.87), kind=kLoop, calls=%fused_computation.5 | loop fusion | flops 5242880 | bytes 7864320 | tf_op jit(solution)/shard_map/convert_element_type | solution.py:180
  202.3 8.5 %fusion.8 = bf16[1024,512]{1,0:T(8,128)(2,1)} fusion(s32[1024]{0:T(1024)S(1)} %select_n.181, bf16[512,5120]{1,0:T(8,128)(2,1)} %copy-done.5, bf16[5120,512]{1,0:T(8,128)(2,1)} %all-gather.5.cloned.1.call-done), kind=kOutput, calls=%fused_computation.18 | convolution fusion | flops 3222536192 | bytes 11538432 | tf_op jit(solution)/shard_map/dot_general | solution.py:155
  210.8 5.1 %all-to-all-start = ((bf16[32,32,512]{2,1,0:T(8,128)(2,1)}), bf16[32,32,512]{2,1,0:T(8,128)(2,1)S(1)}, u32[]{:S(2)}, u32[]{:S(2)}) async-start(bf16[32,32,512]{2,1,0:T(8,128)(2,1)} %bitcast.2), calls=%async_computation.1 | async-start | bytes 2097152 | tf_op jit(solution)/shard_map/all_to_all | solution.py:158
  217.4 2.7 collective-permute-start.9
  222.3 2.5 collective-permute-start.3
  224.8 12.2 %collective-permute-done.9 = bf16[4,320,256]{2,1,0:T(8,128)(2,1)} collective-permute-done((bf16[4,320,256]{2,1,0:T(8,128)(2,1)S(1)}, bf16[4,320,256]{2,1,0:T(8,128)(2,1)}, u32[]{:S(2)}, u32[]{:S(2)}) %collective-permute-start.9) | collective-permute-done | bytes 655392 | tf_op jit(solution)/shard_map/ppermute | solution.py:58
  237.0 2.3 fusion.10
  245.8 3.5 %collective-permute-done.10 = bf16[4,320,256]{2,1,0:T(8,128)(2,1)} collective-permute-done((bf16[4,320,256]{2,1,0:T(8,128)(2,1)}, bf16[4,320,256]{2,1,0:T(8,128)(2,1)}, u32[]{:S(2)}, u32[]{:S(2)}) %collective-permute-start.10) | collective-permute-done | bytes 655392 | tf_op jit(solution)/shard_map/ppermute | solution.py:58
  250.8 2.8 collective-permute-start.13
  256.3 2.5 collective-permute-start.7
  262.1 3.2 %collective-permute-done.6 = bf16[320,256]{1,0:T(8,128)(2,1)S(1)} collective-permute-done((bf16[320,256]{1,0:T(8,128)(2,1)S(1)}, bf16[320,256]{1,0:T(8,128)(2,1)S(1)}, u32[]{:S(2)}, u32[]{:S(2)}) %collective-permute-start.6) | collective-permute-done | bytes 163872 | tf_op jit(solution)/shard_map/ppermute | solution.py:67
  265.6 4.3 %collective-permute-start.14 = (f32[160,512]{1,0:T(8,128)S(1)}, f32[160,512]{1,0:T(8,128)S(1)}, u32[]{:S(2)}, u32[]{:S(2)}) collective-permute-start(f32[160,512]{1,0:T(8,128)S(1)} %get-tuple-element.23), channel_id=1, source_target_pairs={{0,8},{8,0},{1,9},{9,1},{2,10},{10,2},{3,11},{11,3},{4,12},{12,4},... | collective-permute-start | bytes 983048 | tf_op jit(solution)/shard_map/ppermute | solution.py:145
  (118 shorter events, 48.3 us)
Async XLA Ops:
  7.2 55.7 %reduce-scatter.3.cloned.1.call-start = ((), (), s32[]{:S(2)}) async-start(), calls=%async_computation.4 | async-start | bytes 2949120 | tf_op jit(solution)/shard_map/reduce_scatter | solution.py:89
  18.9 89.7 %all-gather.3.cloned.1.call-start = ((), (), s32[]{:S(2)}) async-start(), calls=%async_computation.5 | async-start | bytes 2949120 | tf_op jit(solution)/shard_map/all_gather | solution.py:128
  19.0 45.5 %copy-start.8 = (f32[1280]{0:T(1024)S(1)}, f32[1280]{0:T(1024)}, u32[]{:S(2)}) copy-start(f32[1280]{0:T(1024)} %param.13) | copy-start | bytes 15364
  19.0 45.5 %copy-start.9 = (f32[1280]{0:T(1024)S(1)}, f32[1280]{0:T(1024)}, u32[]{:S(2)}) copy-start(f32[1280]{0:T(1024)} %param.14) | copy-start | bytes 15364
  65.6 109.0 %all-gather.5.cloned.1.call-start = ((), (), s32[]{:S(2)}) async-start(), calls=%async_computation.6 | async-start | bytes 5570560 | tf_op jit(solution)/shard_map/all_gather | solution.py:84
  66.6 5.9 %collective-permute-start.1 = (bf16[160,512]{1,0:T(8,128)(2,1)S(1)}, bf16[160,512]{1,0:T(8,128)(2,1)S(1)}, u32[]{:S(2)}, u32[]{:S(2)}) collective-permute-start(bf16[160,512]{1,0:T(8,128)(2,1)S(1)} %bitcast.104), channel_id=1, source_target_pairs={{0,8},{8,0},{1,9},{9,1},{2,10},{10,2},{3,11},{11,3},{4,12},{12,4},... | collective-permute-start | bytes 491528 | tf_op jit(solution)/shard_map/ppermute | solution.py:82
  78.0 34.8 %all-to-all-start.1 = ((bf16[32,32,512]{2,1,0:T(8,128)(2,1)}), bf16[32,32,512]{2,1,0:T(8,128)(2,1)S(1)}, u32[]{:S(2)}, u32[]{:S(2)}) async-start(bf16[32,32,512]{2,1,0:T(8,128)(2,1)} %bitcast.10), calls=%async_computation.2 | async-start | bytes 2097152 | tf_op jit(solution)/shard_map/all_to_all | solution.py:117
  85.3 187.5 %reduce-scatter.5.cloned.1.call-start = ((), (), s32[]{:S(2)}) async-start(), calls=%async_computation.7 | async-start | bytes 2949120 | tf_op jit(solution)/shard_map/reduce_scatter | solution.py:182
  108.6 77.4 %collective-permute-start = (bf16[256,5120]{1,0:T(8,128)(2,1)}, bf16[256,5120]{1,0:T(8,128)(2,1)}, u32[]{:S(2)}, u32[]{:S(2)}) collective-permute-start(bf16[256,5120]{1,0:T(8,128)(2,1)} %all-gather.3.cloned.1.call-done), channel_id=1, source_target_pairs={{0,8},{8,0},{1,9},{9,1},{2,10},{10,2},{3,11},{11,3},{4,12},{12,4},... | collective-permute-start | bytes 7864328 | tf_op jit(solution)/shard_map/ppermute | solution.py:129
  183.4 11.8 %collective-permute-start.15 = (bf16[256,5120]{1,0:T(8,128)(2,1)}, bf16[256,5120]{1,0:T(8,128)(2,1)}, u32[]{:S(2)}, u32[]{:S(2)}) collective-permute-start(bf16[256,5120]{1,0:T(8,128)(2,1)} %slice.37), channel_id=1, source_target_pairs={{0,8},{8,0},{1,9},{9,1},{2,10},{10,2},{3,11},{11,3},{4,12},{12,4},... | collective-permute-start | bytes 7864328 | tf_op jit(solution)/shard_map/ppermute | solution.py:179
  189.6 26.3 %collective-permute-start.8 = (bf16[4,320,256]{2,1,0:T(8,128)(2,1)S(1)}, bf16[4,320,256]{2,1,0:T(8,128)(2,1)}, u32[]{:S(2)}, u32[]{:S(2)}) collective-permute-start(bf16[4,320,256]{2,1,0:T(8,128)(2,1)S(1)} %dynamic-slice_bitcast_fusion), channel_id=1, source_target_pairs={{0,16},{8,56},{16,32},{24,8},{32,48},{40,24},{48,0},{56,40},{64,80... | collective-permute-start | bytes 1966088 | tf_op jit(solution)/shard_map/ppermute | solution.py:58
  201.5 18.5 %collective-permute-start.2 = (bf16[4,320,256]{2,1,0:T(8,128)(2,1)}, bf16[4,320,256]{2,1,0:T(8,128)(2,1)}, u32[]{:S(2)}, u32[]{:S(2)}) collective-permute-start(bf16[4,320,256]{2,1,0:T(8,128)(2,1)} %dynamic-slice_bitcast_fusion.1), channel_id=1, source_target_pairs={{0,64},{8,200},{16,80},{24,216},{32,96},{40,232},{48,112},{56,248}... | collective-permute-start | bytes 1966088 | tf_op jit(solution)/shard_map/ppermute | solution.py:58
  210.8 34.4 %all-to-all-start = ((bf16[32,32,512]{2,1,0:T(8,128)(2,1)}), bf16[32,32,512]{2,1,0:T(8,128)(2,1)S(1)}, u32[]{:S(2)}, u32[]{:S(2)}) async-start(bf16[32,32,512]{2,1,0:T(8,128)(2,1)} %bitcast.2), calls=%async_computation.1 | async-start | bytes 2097152 | tf_op jit(solution)/shard_map/all_to_all | solution.py:158
  217.4 19.6 %collective-permute-start.9 = (bf16[4,320,256]{2,1,0:T(8,128)(2,1)S(1)}, bf16[4,320,256]{2,1,0:T(8,128)(2,1)}, u32[]{:S(2)}, u32[]{:S(2)}) collective-permute-start(bf16[4,320,256]{2,1,0:T(8,128)(2,1)S(1)} %fusion.11), channel_id=1, source_target_pairs={{0,16},{8,56},{16,32},{24,8},{32,48},{40,24},{48,0},{56,40},{64,80... | collective-permute-start | bytes 1966088 | tf_op jit(solution)/shard_map/ppermute | solution.py:58
  222.3 18.5 %collective-permute-start.3 = (bf16[4,320,256]{2,1,0:T(8,128)(2,1)}, bf16[4,320,256]{2,1,0:T(8,128)(2,1)}, u32[]{:S(2)}, u32[]{:S(2)}) collective-permute-start(bf16[4,320,256]{2,1,0:T(8,128)(2,1)} %fusion.14), channel_id=1, source_target_pairs={{0,64},{8,200},{16,80},{24,216},{32,96},{40,232},{48,112},{56,248}... | collective-permute-start | bytes 1966088 | tf_op jit(solution)/shard_map/ppermute | solution.py:58
  239.3 10.0 %collective-permute-start.10 = (bf16[4,320,256]{2,1,0:T(8,128)(2,1)}, bf16[4,320,256]{2,1,0:T(8,128)(2,1)}, u32[]{:S(2)}, u32[]{:S(2)}) collective-permute-start(bf16[4,320,256]{2,1,0:T(8,128)(2,1)} %fusion.10), channel_id=1, source_target_pairs={{0,16},{8,56},{16,32},{24,8},{32,48},{40,24},{48,0},{56,40},{64,80... | collective-permute-start | bytes 1966088 | tf_op jit(solution)/shard_map/ppermute | solution.py:58
  243.1 12.0 %collective-permute-start.4 = (bf16[4,320,256]{2,1,0:T(8,128)(2,1)}, bf16[4,320,256]{2,1,0:T(8,128)(2,1)S(1)}, u32[]{:S(2)}, u32[]{:S(2)}) collective-permute-start(bf16[4,320,256]{2,1,0:T(8,128)(2,1)} %fusion.13), channel_id=1, source_target_pairs={{0,64},{8,200},{16,80},{24,216},{32,96},{40,232},{48,112},{56,248}... | collective-permute-start | bytes 1966088 | tf_op jit(solution)/shard_map/ppermute | solution.py:58
  250.8 9.1 %collective-permute-start.13 = (bf16[320,256]{1,0:T(8,128)(2,1)S(1)}, bf16[320,256]{1,0:T(8,128)(2,1)S(1)}, u32[]{:S(2)}, u32[]{:S(2)}) collective-permute-start(bf16[320,256]{1,0:T(8,128)(2,1)S(1)} %get-tuple-element.28), channel_id=1, source_target_pairs={{0,128},{64,192},{128,0},{192,64},{1,129},{65,193},{129,1},{193,65... | collective-permute-start | bytes 491528 | tf_op jit(solution)/shard_map/ppermute | solution.py:67
  253.6 6.7 %collective-permute-start.12 = (bf16[320,256]{1,0:T(8,128)(2,1)S(1)}, bf16[320,256]{1,0:T(8,128)(2,1)S(1)}, u32[]{:S(2)}, u32[]{:S(2)}) collective-permute-start(bf16[320,256]{1,0:T(8,128)(2,1)S(1)} %get-tuple-element.29), channel_id=1, source_target_pairs={{0,192},{64,0},{128,64},{192,128},{1,193},{65,1},{129,65},{193,129... | collective-permute-start | bytes 491528 | tf_op jit(solution)/shard_map/ppermute | solution.py:67
  254.5 7.1 %collective-permute-start.11 = (bf16[320,256]{1,0:T(8,128)(2,1)S(1)}, bf16[320,256]{1,0:T(8,128)(2,1)S(1)}, u32[]{:S(2)}, u32[]{:S(2)}) collective-permute-start(bf16[320,256]{1,0:T(8,128)(2,1)S(1)} %get-tuple-element.27), channel_id=1, source_target_pairs={{0,64},{64,128},{128,192},{192,0},{1,65},{65,129},{129,193},{193,1... | collective-permute-start | bytes 491528 | tf_op jit(solution)/shard_map/ppermute | solution.py:67
  256.3 5.8 %collective-permute-start.7 = (bf16[320,256]{1,0:T(8,128)(2,1)S(1)}, bf16[320,256]{1,0:T(8,128)(2,1)S(1)}, u32[]{:S(2)}, u32[]{:S(2)}) collective-permute-start(bf16[320,256]{1,0:T(8,128)(2,1)S(1)} %get-tuple-element.25), channel_id=1, source_target_pairs={{0,32},{16,48},{32,0},{48,16},{1,33},{17,49},{33,1},{49,17},{2,34}... | collective-permute-start | bytes 491528 | tf_op jit(solution)/shard_map/ppermute | solution.py:67
  258.8 6.5 %collective-permute-start.6 = (bf16[320,256]{1,0:T(8,128)(2,1)S(1)}, bf16[320,256]{1,0:T(8,128)(2,1)S(1)}, u32[]{:S(2)}, u32[]{:S(2)}) collective-permute-start(bf16[320,256]{1,0:T(8,128)(2,1)S(1)} %get-tuple-element.26), channel_id=1, source_target_pairs={{0,48},{16,0},{32,16},{48,32},{1,49},{17,1},{33,17},{49,33},{2,50}... | collective-permute-start | bytes 491528 | tf_op jit(solution)/shard_map/ppermute | solution.py:67
  259.9 5.4 %collective-permute-start.5 = (bf16[320,256]{1,0:T(8,128)(2,1)S(1)}, bf16[320,256]{1,0:T(8,128)(2,1)S(1)}, u32[]{:S(2)}, u32[]{:S(2)}) collective-permute-start(bf16[320,256]{1,0:T(8,128)(2,1)S(1)} %get-tuple-element.24), channel_id=1, source_target_pairs={{0,16},{16,32},{32,48},{48,0},{1,17},{17,33},{33,49},{49,1},{2,18}... | collective-permute-start | bytes 491528 | tf_op jit(solution)/shard_map/ppermute | solution.py:67
  265.6 6.2 %collective-permute-start.14 = (f32[160,512]{1,0:T(8,128)S(1)}, f32[160,512]{1,0:T(8,128)S(1)}, u32[]{:S(2)}, u32[]{:S(2)}) collective-permute-start(f32[160,512]{1,0:T(8,128)S(1)} %get-tuple-element.23), channel_id=1, source_target_pairs={{0,8},{8,0},{1,9},{9,1},{2,10},{10,2},{3,11},{11,3},{4,12},{12,4},... | collective-permute-start | bytes 983048 | tf_op jit(solution)/shard_map/ppermute | solution.py:145
  (11 other events, 88.4 us)
Sparse Core Ops, SparseCore 0:
  19.0 43.8 reduce-scatter.2
  65.7 42.7 all-gather.2
  111.6 62.9 all-gather.4
  199.7 38.6 reduce-scatter.4
